TPU v7x, 512 devices: a whole 4x4x16 slice. The times are simulated.
512 devices in a mesh: vr: 16 (over z_hi, y), vc: 32 (over x, z_lo, core).
Axes of the slice: x: 4, y: 4, z: 16 (z_hi: 4, z_lo: 4; z = z_hi * 4 + z_lo), core: 2. Of those that a mesh axis runs over, the one named last changes fastest.
Arguments:
- amplitudes: float32 [1024, 102400], P('vr', 'vc'), may hold values from -6 to 6
- integrals: float32 [5120, 102400], P('vr', 'vc'), may hold values from -0.01953125 to 0.01953125
- mirror_slot: int32 [1024], P('vc'), may hold values from 0 to 31, as said below
Outputs:
- residual: float32 [5120, 1024], P('vr', 'vc')
Inputs may be any that keep to these rules, and one draw needn't show every extreme that they name: Occupied pairs come in 32 blocks of 32; the mirror ji of the pair in block k at position s lies in block (k + 16) mod 32 at position mirror_slot of it, and the relation is mutual: q(q(p)) = p. Within each block the slots form a permutation.
All inputs are finite; a program needn't handle non-finite values.
Results may differ from a plain program's by a relative error of at most 0.000096.
Values sent between devices are 32-bit elements; how exact they have to be, the bound alone decides.
No kernel may reach another device: no remote copies, remote signals or barrier semaphores. Data moves between devices by JAX's collectives and lax.ppermute only.
A program may use at most 64 MiB of HBM per device.

v0:
```python
import jax
import jax.numpy as jnp
from jax import lax
from jax.sharding import PartitionSpec as P


def from_partner(value, axis, bit):
    mask = 2**bit
    pairs = [(source, source ^ mask) for source in range(lax.axis_size(axis))]
    return lax.ppermute(value, axis, pairs)


def block_product(integrals, pieces):
    return lax.dot_general(
        integrals,
        pieces,
        (((1,), (1,)), ((), ())),
        precision=lax.Precision.HIGHEST,
        preferred_element_type=jnp.float32,
    )


def local(amplitudes, integrals, mirror_slot):
    partial_value = block_product(integrals, lax.all_gather(amplitudes, "vr", axis=0, tiled=True))
    group_count = lax.axis_size("vc")
    summed = lax.psum_scatter(partial_value, "vc", scatter_dimension=1, tiled=True)
    partner = from_partner(summed, "vc", group_count.bit_length() - 2)
    return summed - jnp.take(partner, mirror_slot, axis=1)


def solution(mesh):
    in_specs = (P("vr", "vc"), P("vr", "vc"), P("vc"))
    out_specs = P("vr", "vc")
    return jax.shard_map(local, mesh=mesh, in_specs=in_specs, out_specs=out_specs, check_vma=False)
```

profile of v0, /device:TPU:8, one launch (start us, length us, event | category | flops | bytes accessed | tf_op | source)
XLA Modules:
  0.0 519.6 jit_solution(8294091220145129808)
XLA Ops:
  6.5 0.0 all-gather.2.cloned.1.call-start
  6.5 0.7 all-gather.2.cloned.1.call-update
  7.3 0.0 copy-start
  7.3 0.0 reduce-scatter.2.cloned.1.call-start
  7.3 319.9 %all-gather.2.cloned.1.call-done = f32[1024,3200]{1,0:T(8,128)} async-done(((f32[64,3200]{1,0:T(8,128)}), f32[1024,3200]{1,0:T(8,128)}) %all-gather.2.cloned.1.call-update) | async-done | bytes 13107216 | tf_op jit(solution)/shard_map/all_gather | solution.py:24
  327.2 27.0 %fusion = f32[320,1024]{0,1:T(8,128)} fusion(f32[320,3200]{1,0:T(8,128)} %param.4, f32[1024,3200]{1,0:T(8,128)} %all-gather.2.cloned.1.call-done), kind=kOutput, calls=%fused_computation.5 | convolution fusion | flops 12582912000 | bytes 18513920 | tf_op jit(solution)/shard_map/dot_general | solution.py:14
  354.2 0.0 reduce-scatter.2.cloned.1.call-update
  354.2 0.0 copy-done
  354.2 148.7 %reduce-scatter.2.cloned.1.call-done = f32[320,32]{0,1:T(8,128)} async-done(((f32[320,1024]{0,1:T(8,128)}), f32[320,32]{0,1:T(8,128)}) %reduce-scatter.2.cloned.1.call-update) | async-done | bytes 40976 | tf_op jit(solution)/shard_map/reduce_scatter | solution.py:26
  502.9 1.9 collective-permute-start
  504.9 5.8 %collective-permute-done = f32[320,32]{0,1:T(8,128)S(1)} collective-permute-done((f32[320,32]{0,1:T(8,128)}, f32[320,32]{0,1:T(8,128)S(1)}, u32[]{:S(2)}, u32[]{:S(2)}) %collective-permute-start) | collective-permute-done | bytes 40992 | tf_op jit(solution)/shard_map/ppermute | solution.py:10
  510.6 0.6 gather_fusion
  511.2 1.5 bitcast_subtract_fusion
  (3 shorter events, 0.0 us)
Async XLA Ops:
  6.5 320.7 %all-gather.2.cloned.1.call-start = ((), (), s32[]{:S(2)}) async-start(), calls=%async_computation.1 | async-start | bytes 13926400 | tf_op jit(solution)/shard_map/all_gather | solution.py:24
  7.3 347.0 %copy-start = (s32[32]{0:T(128)S(1)}, s32[32]{0:T(128)}, u32[]{:S(2)}) copy-start(s32[32]{0:T(128)} %param.5) | copy-start | bytes 388
  7.3 495.7 %reduce-scatter.2.cloned.1.call-start = ((), (), s32[]{:S(2)}) async-start(), calls=%async_computation.2 | async-start | bytes 1622016 | tf_op jit(solution)/shard_map/reduce_scatter | solution.py:26
  502.9 7.7 %collective-permute-start = (f32[320,32]{0,1:T(8,128)}, f32[320,32]{0,1:T(8,128)S(1)}, u32[]{:S(2)}, u32[]{:S(2)}) collective-permute-start(f32[320,32]{0,1:T(8,128)} %reduce-scatter.2.cloned.1.call-done), channel_id=1, source_target_pairs={{0,16},{1,17},{2,18},{3,19},{4,20},{5,21},{6,22},{7,23},{8,24},{9,... | collective-permute-start | bytes 122888 | tf_op jit(solution)/shard_map/ppermute | solution.py:10
Sparse Core Ops, SparseCore 0:
  10.4 316.7 all-gather.1
  354.3 148.5 reduce-scatter.1
where the time goes:
time: 520 us
  waiting for transfers between devices  475 us (91%)
  matrix products  27 us (5%)
  between operations  13.4 us (3%)
    all_gather x1, waiting for transfers between devices, local(): lax.all_gather(amplitudes, 'vr', axis=0, tiled=True)  320 us
    reduce_scatter x1, waiting for transfers between devices, local(): lax.psum_scatter(partial_value, 'vc', scatter_dimension=1, tiled=True)  149 us
    dot_general x1, matrix products, block_product(): lax.dot_general(integrals, pieces, (((1,), (1,)), ((), ())), precision=la...  27 us
  transfers between devices with their start and end apart: 3, of which 3 were waited for; matrix products, arithmetic and copies ran while one was open for 0% of the time, Pallas kernels for 0%

commit v1 on v0

v1 whole, which is shorter than its diff:
```python
import jax
import jax.numpy as jnp
from jax import lax
from jax.sharding import PartitionSpec as P

FIRST = (9, 0, 8, 1)
HIGH = lax.Precision.HIGH
HIGHEST = lax.Precision.HIGHEST


def move_z(value, step):
    return lax.ppermute(value, "vr", [(4 * z + y, 4 * ((z + step) % 4) + y) for z in range(4) for y in range(4)])


def move_y(value, step):
    return lax.ppermute(value, "vr", [(4 * z + y, 4 * z + (y + step) % 4) for z in range(4) for y in range(4)])


def move_x(value, step):
    return lax.ppermute(value, "vc", [(8 * x + r, 8 * ((x + step) % 4) + r) for x in range(4) for r in range(8)])


def move_low(value, step):
    pairs = [(8 * x + 2 * k + c, 8 * x + 2 * ((k + step) % 4) + c) for x in range(4) for k in range(4) for c in range(2)]
    return lax.ppermute(value, "vc", pairs)


def move_core(value):
    return lax.ppermute(value, "vc", [(c, c ^ 1) for c in range(32)])


def slots_of_my_block(mirror_slot):
    pairs = []
    for z in range(4):
        for y in range(4):
            block = FIRST[z] + 2 * y
            for i in range(16):
                pairs.append((32 * i + block, 32 * (4 * z + y) + i))
                pairs.append((32 * i + block + 16, 32 * (4 * z + y) + i + 16))
    return lax.ppermute(mirror_slot, ("vr", "vc"), pairs)


def all_y(value):
    return jnp.concatenate([value, move_y(value, 3), move_y(value, 2), move_y(value, 1)], 0)


def rolled(blocks, start):
    n = blocks.shape[0]
    return lax.dynamic_slice_in_dim(jnp.concatenate([blocks, blocks], 0), (n - start) % n, n, 0)


def local(amplitudes, integrals, mirror_slot):
    vr, vc = lax.axis_index("vr"), lax.axis_index("vc")
    z, y = vr // 4, vr % 4
    x, low, core = vc // 8, vc // 2 % 4, vc % 2
    iota = jnp.arange(32, dtype=jnp.int32)

    slots = slots_of_my_block(mirror_slot)
    up = lax.dynamic_slice_in_dim(amplitudes, 32 * (z // 2), 32, 0)
    down = lax.dynamic_slice_in_dim(amplitudes, 32 * (1 - z // 2), 32, 0)
    below, above = move_z(up, 1), move_z(down, 3)
    middle = (z == 1) | (z == 2)
    first, second = jnp.where(middle, below, above), jnp.where(middle, above, below)
    chosen = jnp.where(vc < 16, slots[:, None] == iota[None, :], slots[None, :] == iota[:, None])
    mine = first - jnp.dot(chosen.astype(jnp.float32), second, precision=HIGHEST)

    from_below, from_above = move_z(mine, 1), move_z(mine, 3)
    far = jnp.concatenate([move_z(from_below[:16], 1), move_z(from_above[16:], 3)], 0)

    def product(value):
        return lax.dot_general(value, integrals, (((1,), (1,)), ((), ())), precision=HIGH, preferred_element_type=jnp.float32)

    parts = [rolled(product(all_y(v)).reshape(4, 32, 320), y) for v in (mine, from_above, far, from_below)]
    parts = rolled(jnp.stack(parts), z)

    even, odd = jnp.stack([parts[1], parts[2]]), jnp.stack([parts[3], parts[0]])
    total = jnp.where(core == 0, even, odd) + move_core(jnp.where(core == 0, odd, even))
    odd_x = x % 2 == 1
    kept, given = jnp.where(odd_x, total[1], total[0]), jnp.where(odd_x, total[0], total[1])
    total = kept + move_x(kept, 2) + move_x(given, 1) + move_x(given, 3)
    at = [lax.dynamic_index_in_dim(total, (low + d) % 4, 0, False) for d in range(4)]
    total = at[0] + move_low(at[1], 1) + move_low(at[2], 2) + move_low(at[3], 3)

    slot = jnp.where(vc < 16, iota, mirror_slot)
    signed = jnp.where(slot[:, None] == iota[None, :], jnp.where(vc < 16, 1.0, -1.0), 0.0)
    return jnp.dot(signed, total, precision=HIGHEST).T


def solution(mesh):
    in_specs = (P("vr", "vc"), P("vr", "vc"), P("vc"))
    out_specs = P("vr", "vc")
    return jax.shard_map(local, mesh=mesh, in_specs=in_specs, out_specs=out_specs, check_vma=False)
```

time: 520 us -> 216 us (0.42)
  the two profiles are of different devices: /device:TPU:8 before, /device:TPU:352 now
where the time goes in v1:
time: 216 us
  starting transfers between devices  117 us (54%)
  waiting for transfers between devices  82.6 us (38%)
  matrix products  13.2 us (6%)
    ppermute x12, starting transfers between devices, move_y(): lax.ppermute(value, 'vr', [(4 * z + y, 4 * z + (y + step) % 4) for z in r...  40.4 us
    ppermute x1, waiting for transfers between devices, slots_of_my_block(): return lax.ppermute(mirror_slot, ('vr', 'vc'), pairs)  31.6 us
    ppermute x6, starting transfers between devices, move_z(): lax.ppermute(value, 'vr', [(4 * z + y, 4 * ((z + step) % 4) + y) for z in...  29.1 us
    ppermute x3, starting transfers between devices, move_x(): lax.ppermute(value, 'vc', [(8 * x + r, 8 * ((x + step) % 4) + r) for x in...  19.6 us
    ppermute x6, waiting for transfers between devices, move_z(): lax.ppermute(value, 'vr', [(4 * z + y, 4 * ((z + step) % 4) + y) for z in...  19.6 us
    ppermute x3, starting transfers between devices, move_low(): return lax.ppermute(value, 'vc', pairs)  19.3 us
    ppermute x12, waiting for transfers between devices, move_y(): lax.ppermute(value, 'vr', [(4 * z + y, 4 * z + (y + step) % 4) for z in r...  18.2 us
    dot_general x4, matrix products, product(): lax.dot_general(value, integrals, (((1,), (1,)), ((), ())), precision=HIG...  11.9 us
  transfers between devices with their start and end apart: 26, of which 12 were waited for; matrix products, arithmetic and copies ran while one was open for 5% of the time, Pallas kernels for 0%

profile of v1, /device:TPU:352, one launch (start us, length us, event | category | flops | bytes accessed | tf_op | source)
XLA Modules:
  0.0 215.5 jit_solution(4774746040109357992)
XLA Ops:
  1.2 4.3 %collective-permute-start = (f32[32,3200]{1,0:T(8,128)S(1)}, f32[32,3200]{1,0:T(8,128)S(1)}, u32[]{:S(2)}, u32[]{:S(2)}) collective-permute-start(f32[32,3200]{1,0:T(8,128)S(1)} %get-tuple-element.8), channel_id=1, source_target_pairs={{0,128},{32,160},{64,192},{96,224},{128,256},{160,288},{192,320},{... | collective-permute-start | bytes 1228808 | tf_op jit(solution)/shard_map/ppermute | solution.py:12
  5.5 5.5 %collective-permute-start.1 = (f32[32,3200]{1,0:T(8,128)S(1)}, f32[32,3200]{1,0:T(8,128)S(1)}, u32[]{:S(2)}, u32[]{:S(2)}) collective-permute-start(f32[32,3200]{1,0:T(8,128)S(1)} %get-tuple-element.7), channel_id=1, source_target_pairs={{0,384},{32,416},{64,448},{96,480},{128,0},{160,32},{192,64},{224,... | collective-permute-start | bytes 1228808 | tf_op jit(solution)/shard_map/ppermute | solution.py:12
  11.0 6.6 %collective-permute-start.2 = (s32[32]{0:T(128)S(1)}, s32[32]{0:T(128)S(1)}, u32[]{:S(2)}, u32[]{:S(2)}) collective-permute-start(s32[32]{0:T(128)S(1)} %copy-done.1), channel_id=1, source_target_pairs={{9,0},{25,16},{41,1},{57,17},{73,2},{89,18},{105,3},{121,19},{137,... | collective-permute-start | bytes 392 | tf_op jit(solution)/shard_map/ppermute | solution.py:40
  17.6 31.6 %collective-permute-done.2 = s32[32]{0:T(128)S(1)} collective-permute-done((s32[32]{0:T(128)S(1)}, s32[32]{0:T(128)S(1)}, u32[]{:S(2)}, u32[]{:S(2)}) %collective-permute-start.2) | collective-permute-done | bytes 160 | tf_op jit(solution)/shard_map/ppermute | solution.py:40
  49.6 5.3 %collective-permute-start.10 = (f32[32,3200]{1,0:T(8,128)S(1)}, f32[32,3200]{1,0:T(8,128)S(1)}, u32[]{:S(2)}, u32[]{:S(2)}) collective-permute-start(f32[32,3200]{1,0:T(8,128)S(1)} %select_subtract_fusion), channel_id=1, source_target_pairs={{0,128},{32,160},{64,192},{96,224},{128,256},{160,288},{192,320},{... | collective-permute-start | bytes 1228808 | tf_op jit(solution)/shard_map/ppermute | solution.py:12
  54.9 4.5 %collective-permute-start.6 = (f32[32,3200]{1,0:T(8,128)S(1)}, f32[32,3200]{1,0:T(8,128)S(1)}, u32[]{:S(2)}, u32[]{:S(2)}) collective-permute-start(f32[32,3200]{1,0:T(8,128)S(1)} %select_subtract_fusion), channel_id=1, source_target_pairs={{0,384},{32,416},{64,448},{96,480},{128,0},{160,32},{192,64},{224,... | collective-permute-start | bytes 1228808 | tf_op jit(solution)/shard_map/ppermute | solution.py:12
  59.4 3.0 %collective-permute-start.3 = (f32[32,3200]{1,0:T(8,128)S(1)}, f32[32,3200]{1,0:T(8,128)S(1)}, u32[]{:S(2)}, u32[]{:S(2)}) collective-permute-start(f32[32,3200]{1,0:T(8,128)S(1)} %select_subtract_fusion), channel_id=1, source_target_pairs={{0,96},{32,0},{64,32},{96,64},{128,224},{160,128},{192,160},{224,1... | collective-permute-start | bytes 1228808 | tf_op jit(solution)/shard_map/ppermute | solution.py:16
  65.0 2.9 %collective-permute-start.5 = (f32[32,3200]{1,0:T(8,128)S(1)}, f32[32,3200]{1,0:T(8,128)S(1)}, u32[]{:S(2)}, u32[]{:S(2)}) collective-permute-start(f32[32,3200]{1,0:T(8,128)S(1)} %select_subtract_fusion), channel_id=1, source_target_pairs={{0,32},{32,64},{64,96},{96,0},{128,160},{160,192},{192,224},{224,1... | collective-permute-start | bytes 1228808 | tf_op jit(solution)/shard_map/ppermute | solution.py:16
  68.0 18.9 %collective-permute-done.10 = f32[32,3200]{1,0:T(8,128)S(1)} collective-permute-done((f32[32,3200]{1,0:T(8,128)S(1)}, f32[32,3200]{1,0:T(8,128)S(1)}, u32[]{:S(2)}, u32[]{:S(2)}) %collective-permute-start.10) | collective-permute-done | bytes 409632 | tf_op jit(solution)/shard_map/ppermute | solution.py:12
  86.9 7.3 %collective-permute-start.11 = (f32[16,3200]{1,0:T(8,128)S(1)}, f32[16,3200]{1,0:T(8,128)S(1)}, u32[]{:S(2)}, u32[]{:S(2)}) collective-permute-start(f32[16,3200]{1,0:T(8,128)S(1)} %slice.29), channel_id=1, source_target_pairs={{0,128},{32,160},{64,192},{96,224},{128,256},{160,288},{192,320},{... | collective-permute-start | bytes 614408 | tf_op jit(solution)/shard_map/ppermute | solution.py:12
  97.2 4.8 %collective-permute-start.7 = (f32[32,3200]{1,0:T(8,128)S(1)}, f32[32,3200]{1,0:T(8,128)S(1)}, u32[]{:S(2)}, u32[]{:S(2)}) collective-permute-start(f32[32,3200]{1,0:T(8,128)S(1)} %collective-permute-done.6), channel_id=1, source_target_pairs={{0,96},{32,0},{64,32},{96,64},{128,224},{160,128},{192,160},{224,1... | collective-permute-start | bytes 1228808 | tf_op jit(solution)/shard_map/ppermute | solution.py:16
  106.7 4.6 %fusion = f32[128,320]{1,0:T(8,128)S(1)} fusion(f32[320,3200]{1,0:T(8,128)} %param.4, f32[32,3200]{1,0:T(8,128)S(1)} %collective-permute-done.5, f32[32,3200]{1,0:T(8,128)S(1)} %collective-permute-done.4, f32[32,3200]{1,0:T(8,128)S(1)} %collective-permute-done.3, f32[32,3200]{1,0:T(8,128)S(1)} %select_subtract_fusion), kind=kOutput, calls=%fused_computation | convolution fusion | flops 787660800 | bytes 5898240 | tf_op jit(solution)/shard_map/dot_general | solution.py:71
  111.4 4.3 %collective-permute-start.16 = (f32[32,3200]{1,0:T(8,128)S(1)}, f32[32,3200]{1,0:T(8,128)S(1)}, u32[]{:S(2)}, u32[]{:S(2)}) collective-permute-start(f32[32,3200]{1,0:T(8,128)S(1)} %collective-permute-done.10), channel_id=1, source_target_pairs={{0,96},{32,0},{64,32},{96,64},{128,224},{160,128},{192,160},{224,1... | collective-permute-start | bytes 1228808 | tf_op jit(solution)/shard_map/ppermute | solution.py:16
  115.7 4.2 %collective-permute-start.17 = (f32[32,3200]{1,0:T(8,128)S(1)}, f32[32,3200]{1,0:T(8,128)S(1)}, u32[]{:S(2)}, u32[]{:S(2)}) collective-permute-start(f32[32,3200]{1,0:T(8,128)S(1)} %collective-permute-done.10), channel_id=1, source_target_pairs={{0,64},{32,96},{64,0},{96,32},{128,192},{160,224},{192,128},{224,1... | collective-permute-start | bytes 1228808 | tf_op jit(solution)/shard_map/ppermute | solution.py:16
  121.9 5.1 %collective-permute-start.13 = (f32[32,3200]{1,0:T(8,128)S(1)}, f32[32,3200]{1,0:T(8,128)S(1)}, u32[]{:S(2)}, u32[]{:S(2)}) collective-permute-start(f32[32,3200]{1,0:T(8,128)S(1)} %get-tuple-element.11), channel_id=1, source_target_pairs={{0,96},{32,0},{64,32},{96,64},{128,224},{160,128},{192,160},{224,1... | collective-permute-start | bytes 1228808 | tf_op jit(solution)/shard_map/ppermute | solution.py:16
  134.5 4.5 %collective-permute-start.15 = (f32[32,3200]{1,0:T(8,128)S(1)}, f32[32,3200]{1,0:T(8,128)S(1)}, u32[]{:S(2)}, u32[]{:S(2)}) collective-permute-start(f32[32,3200]{1,0:T(8,128)S(1)} %get-tuple-element.11), channel_id=1, source_target_pairs={{0,32},{32,64},{64,96},{96,0},{128,160},{160,192},{192,224},{224,1... | collective-permute-start | bytes 1228808 | tf_op jit(solution)/shard_map/ppermute | solution.py:16
  139.0 8.1 %collective-permute-done.18 = f32[32,3200]{1,0:T(8,128)S(1)} collective-permute-done((f32[32,3200]{1,0:T(8,128)S(1)}, f32[32,3200]{1,0:T(8,128)S(1)}, u32[]{:S(2)}, u32[]{:S(2)}) %collective-permute-start.18) | collective-permute-done | bytes 409632 | tf_op jit(solution)/shard_map/ppermute | solution.py:16
  151.7 5.5 %collective-permute-done.15 = f32[32,3200]{1,0:T(8,128)S(1)} collective-permute-done((f32[32,3200]{1,0:T(8,128)S(1)}, f32[32,3200]{1,0:T(8,128)S(1)}, u32[]{:S(2)}, u32[]{:S(2)}) %collective-permute-start.15) | collective-permute-done | bytes 409632 | tf_op jit(solution)/shard_map/ppermute | solution.py:16
  163.9 5.8 %collective-permute-start.20 = (f32[4,32,320]{2,1,0:T(8,128)S(1)}, f32[4,32,320]{2,1,0:T(8,128)S(1)}, u32[]{:S(2)}, u32[]{:S(2)}) collective-permute-start(f32[4,32,320]{2,1,0:T(8,128)S(1)} %get-tuple-element.9), channel_id=1, source_target_pairs={{0,16},{1,17},{2,18},{3,19},{4,20},{5,21},{6,22},{7,23},{8,24},{9,... | collective-permute-start | bytes 491528 | tf_op jit(solution)/shard_map/ppermute | solution.py:20
  169.7 11.4 %collective-permute-start.21 = (f32[4,32,320]{2,1,0:T(8,128)S(1)}, f32[4,32,320]{2,1,0:T(8,128)S(1)}, u32[]{:S(2)}, u32[]{:S(2)}) collective-permute-start(f32[4,32,320]{2,1,0:T(8,128)S(1)} %get-tuple-element.10), channel_id=1, source_target_pairs={{0,8},{1,9},{2,10},{3,11},{4,12},{5,13},{6,14},{7,15},{8,16},{9,17... | collective-permute-start | bytes 491528 | tf_op jit(solution)/shard_map/ppermute | solution.py:20
  183.6 2.9 %collective-permute-done.21 = f32[4,32,320]{2,1,0:T(8,128)S(1)} collective-permute-done((f32[4,32,320]{2,1,0:T(8,128)S(1)}, f32[4,32,320]{2,1,0:T(8,128)S(1)}, u32[]{:S(2)}, u32[]{:S(2)}) %collective-permute-start.21) | collective-permute-done | bytes 163872 | tf_op jit(solution)/shard_map/ppermute | solution.py:20
  186.5 2.9 %collective-permute-done.22 = f32[4,32,320]{2,1,0:T(8,128)S(1)} collective-permute-done((f32[4,32,320]{2,1,0:T(8,128)S(1)}, f32[4,32,320]{2,1,0:T(8,128)S(1)}, u32[]{:S(2)}, u32[]{:S(2)}) %collective-permute-start.22) | collective-permute-done | bytes 163872 | tf_op jit(solution)/shard_map/ppermute | solution.py:20
  191.4 15.5 %collective-permute-start.24 = (f32[32,320]{1,0:T(8,128)S(1)}, f32[32,320]{1,0:T(8,128)S(1)}, u32[]{:S(2)}, u32[]{:S(2)}) collective-permute-start(f32[32,320]{1,0:T(8,128)S(1)} %get-tuple-element.17), channel_id=1, source_target_pairs={{0,4},{1,5},{2,6},{3,7},{4,0},{5,1},{6,2},{7,3},{8,12},{9,13},{10,... | collective-permute-start | bytes 122888 | tf_op jit(solution)/shard_map/ppermute | solution.py:25
  208.9 5.7 %collective-permute-done.25 = f32[32,320]{1,0:T(8,128)S(1)} collective-permute-done((f32[32,320]{1,0:T(8,128)S(1)}, f32[32,320]{1,0:T(8,128)S(1)}, u32[]{:S(2)}, u32[]{:S(2)}) %collective-permute-start.25) | collective-permute-done | bytes 40992 | tf_op jit(solution)/shard_map/ppermute | solution.py:25
  (61 shorter events, 39.6 us)
Async XLA Ops:
  1.2 48.0 %collective-permute-start = (f32[32,3200]{1,0:T(8,128)S(1)}, f32[32,3200]{1,0:T(8,128)S(1)}, u32[]{:S(2)}, u32[]{:S(2)}) collective-permute-start(f32[32,3200]{1,0:T(8,128)S(1)} %get-tuple-element.8), channel_id=1, source_target_pairs={{0,128},{32,160},{64,192},{96,224},{128,256},{160,288},{192,320},{... | collective-permute-start | bytes 1228808 | tf_op jit(solution)/shard_map/ppermute | solution.py:12
  5.5 43.7 %collective-permute-start.1 = (f32[32,3200]{1,0:T(8,128)S(1)}, f32[32,3200]{1,0:T(8,128)S(1)}, u32[]{:S(2)}, u32[]{:S(2)}) collective-permute-start(f32[32,3200]{1,0:T(8,128)S(1)} %get-tuple-element.7), channel_id=1, source_target_pairs={{0,384},{32,416},{64,448},{96,480},{128,0},{160,32},{192,64},{224,... | collective-permute-start | bytes 1228808 | tf_op jit(solution)/shard_map/ppermute | solution.py:12
  11.0 38.3 %collective-permute-start.2 = (s32[32]{0:T(128)S(1)}, s32[32]{0:T(128)S(1)}, u32[]{:S(2)}, u32[]{:S(2)}) collective-permute-start(s32[32]{0:T(128)S(1)} %copy-done.1), channel_id=1, source_target_pairs={{9,0},{25,16},{41,1},{57,17},{73,2},{89,18},{105,3},{121,19},{137,... | collective-permute-start | bytes 392 | tf_op jit(solution)/shard_map/ppermute | solution.py:40
  49.6 37.3 %collective-permute-start.10 = (f32[32,3200]{1,0:T(8,128)S(1)}, f32[32,3200]{1,0:T(8,128)S(1)}, u32[]{:S(2)}, u32[]{:S(2)}) collective-permute-start(f32[32,3200]{1,0:T(8,128)S(1)} %select_subtract_fusion), channel_id=1, source_target_pairs={{0,128},{32,160},{64,192},{96,224},{128,256},{160,288},{192,320},{... | collective-permute-start | bytes 1228808 | tf_op jit(solution)/shard_map/ppermute | solution.py:12
  54.9 39.9 %collective-permute-start.6 = (f32[32,3200]{1,0:T(8,128)S(1)}, f32[32,3200]{1,0:T(8,128)S(1)}, u32[]{:S(2)}, u32[]{:S(2)}) collective-permute-start(f32[32,3200]{1,0:T(8,128)S(1)} %select_subtract_fusion), channel_id=1, source_target_pairs={{0,384},{32,416},{64,448},{96,480},{128,0},{160,32},{192,64},{224,... | collective-permute-start | bytes 1228808 | tf_op jit(solution)/shard_map/ppermute | solution.py:12
  59.4 37.8 %collective-permute-start.3 = (f32[32,3200]{1,0:T(8,128)S(1)}, f32[32,3200]{1,0:T(8,128)S(1)}, u32[]{:S(2)}, u32[]{:S(2)}) collective-permute-start(f32[32,3200]{1,0:T(8,128)S(1)} %select_subtract_fusion), channel_id=1, source_target_pairs={{0,96},{32,0},{64,32},{96,64},{128,224},{160,128},{192,160},{224,1... | collective-permute-start | bytes 1228808 | tf_op jit(solution)/shard_map/ppermute | solution.py:16
  62.5 39.5 %collective-permute-start.4 = (f32[32,3200]{1,0:T(8,128)S(1)}, f32[32,3200]{1,0:T(8,128)S(1)}, u32[]{:S(2)}, u32[]{:S(2)}) collective-permute-start(f32[32,3200]{1,0:T(8,128)S(1)} %select_subtract_fusion), channel_id=1, source_target_pairs={{0,64},{32,96},{64,0},{96,32},{128,192},{160,224},{192,128},{224,1... | collective-permute-start | bytes 1228808 | tf_op jit(solution)/shard_map/ppermute | solution.py:16
  65.0 38.9 %collective-permute-start.5 = (f32[32,3200]{1,0:T(8,128)S(1)}, f32[32,3200]{1,0:T(8,128)S(1)}, u32[]{:S(2)}, u32[]{:S(2)}) collective-permute-start(f32[32,3200]{1,0:T(8,128)S(1)} %select_subtract_fusion), channel_id=1, source_target_pairs={{0,32},{32,64},{64,96},{96,0},{128,160},{160,192},{192,224},{224,1... | collective-permute-start | bytes 1228808 | tf_op jit(solution)/shard_map/ppermute | solution.py:16
  86.9 24.5 %collective-permute-start.11 = (f32[16,3200]{1,0:T(8,128)S(1)}, f32[16,3200]{1,0:T(8,128)S(1)}, u32[]{:S(2)}, u32[]{:S(2)}) collective-permute-start(f32[16,3200]{1,0:T(8,128)S(1)} %slice.29), channel_id=1, source_target_pairs={{0,128},{32,160},{64,192},{96,224},{128,256},{160,288},{192,320},{... | collective-permute-start | bytes 614408 | tf_op jit(solution)/shard_map/ppermute | solution.py:12
  94.8 20.9 %collective-permute-start.12 = (f32[16,3200]{1,0:T(8,128)S(1)}, f32[16,3200]{1,0:T(8,128)S(1)}, u32[]{:S(2)}, u32[]{:S(2)}) collective-permute-start(f32[16,3200]{1,0:T(8,128)S(1)} %slice.30), channel_id=1, source_target_pairs={{0,384},{32,416},{64,448},{96,480},{128,0},{160,32},{192,64},{224,... | collective-permute-start | bytes 614408 | tf_op jit(solution)/shard_map/ppermute | solution.py:12
  97.2 22.8 %collective-permute-start.7 = (f32[32,3200]{1,0:T(8,128)S(1)}, f32[32,3200]{1,0:T(8,128)S(1)}, u32[]{:S(2)}, u32[]{:S(2)}) collective-permute-start(f32[32,3200]{1,0:T(8,128)S(1)} %collective-permute-done.6), channel_id=1, source_target_pairs={{0,96},{32,0},{64,32},{96,64},{128,224},{160,128},{192,160},{224,1... | collective-permute-start | bytes 1228808 | tf_op jit(solution)/shard_map/ppermute | solution.py:16
  102.0 19.9 %collective-permute-start.8 = (f32[32,3200]{1,0:T(8,128)S(1)}, f32[32,3200]{1,0:T(8,128)S(1)}, u32[]{:S(2)}, u32[]{:S(2)}) collective-permute-start(f32[32,3200]{1,0:T(8,128)S(1)} %collective-permute-done.6), channel_id=1, source_target_pairs={{0,64},{32,96},{64,0},{96,32},{128,192},{160,224},{192,128},{224,1... | collective-permute-start | bytes 1228808 | tf_op jit(solution)/shard_map/ppermute | solution.py:16
  103.9 25.6 %collective-permute-start.9 = (f32[32,3200]{1,0:T(8,128)S(1)}, f32[32,3200]{1,0:T(8,128)S(1)}, u32[]{:S(2)}, u32[]{:S(2)}) collective-permute-start(f32[32,3200]{1,0:T(8,128)S(1)} %collective-permute-done.6), channel_id=1, source_target_pairs={{0,32},{32,64},{64,96},{96,0},{128,160},{160,192},{192,224},{224,1... | collective-permute-start | bytes 1228808 | tf_op jit(solution)/shard_map/ppermute | solution.py:16
  111.4 23.1 %collective-permute-start.16 = (f32[32,3200]{1,0:T(8,128)S(1)}, f32[32,3200]{1,0:T(8,128)S(1)}, u32[]{:S(2)}, u32[]{:S(2)}) collective-permute-start(f32[32,3200]{1,0:T(8,128)S(1)} %collective-permute-done.10), channel_id=1, source_target_pairs={{0,96},{32,0},{64,32},{96,64},{128,224},{160,128},{192,160},{224,1... | collective-permute-start | bytes 1228808 | tf_op jit(solution)/shard_map/ppermute | solution.py:16
  115.7 23.3 %collective-permute-start.17 = (f32[32,3200]{1,0:T(8,128)S(1)}, f32[32,3200]{1,0:T(8,128)S(1)}, u32[]{:S(2)}, u32[]{:S(2)}) collective-permute-start(f32[32,3200]{1,0:T(8,128)S(1)} %collective-permute-done.10), channel_id=1, source_target_pairs={{0,64},{32,96},{64,0},{96,32},{128,192},{160,224},{192,128},{224,1... | collective-permute-start | bytes 1228808 | tf_op jit(solution)/shard_map/ppermute | solution.py:16
  120.0 27.1 %collective-permute-start.18 = (f32[32,3200]{1,0:T(8,128)S(1)}, f32[32,3200]{1,0:T(8,128)S(1)}, u32[]{:S(2)}, u32[]{:S(2)}) collective-permute-start(f32[32,3200]{1,0:T(8,128)S(1)} %collective-permute-done.10), channel_id=1, source_target_pairs={{0,32},{32,64},{64,96},{96,0},{128,160},{160,192},{192,224},{224,1... | collective-permute-start | bytes 1228808 | tf_op jit(solution)/shard_map/ppermute | solution.py:16
  121.9 27.6 %collective-permute-start.13 = (f32[32,3200]{1,0:T(8,128)S(1)}, f32[32,3200]{1,0:T(8,128)S(1)}, u32[]{:S(2)}, u32[]{:S(2)}) collective-permute-start(f32[32,3200]{1,0:T(8,128)S(1)} %get-tuple-element.11), channel_id=1, source_target_pairs={{0,96},{32,0},{64,32},{96,64},{128,224},{160,128},{192,160},{224,1... | collective-permute-start | bytes 1228808 | tf_op jit(solution)/shard_map/ppermute | solution.py:16
  129.6 22.1 %collective-permute-start.14 = (f32[32,3200]{1,0:T(8,128)S(1)}, f32[32,3200]{1,0:T(8,128)S(1)}, u32[]{:S(2)}, u32[]{:S(2)}) collective-permute-start(f32[32,3200]{1,0:T(8,128)S(1)} %get-tuple-element.11), channel_id=1, source_target_pairs={{0,64},{32,96},{64,0},{96,32},{128,192},{160,224},{192,128},{224,1... | collective-permute-start | bytes 1228808 | tf_op jit(solution)/shard_map/ppermute | solution.py:16
  134.5 22.7 %collective-permute-start.15 = (f32[32,3200]{1,0:T(8,128)S(1)}, f32[32,3200]{1,0:T(8,128)S(1)}, u32[]{:S(2)}, u32[]{:S(2)}) collective-permute-start(f32[32,3200]{1,0:T(8,128)S(1)} %get-tuple-element.11), channel_id=1, source_target_pairs={{0,32},{32,64},{64,96},{96,0},{128,160},{160,192},{192,224},{224,1... | collective-permute-start | bytes 1228808 | tf_op jit(solution)/shard_map/ppermute | solution.py:16
  163.9 19.7 %collective-permute-start.20 = (f32[4,32,320]{2,1,0:T(8,128)S(1)}, f32[4,32,320]{2,1,0:T(8,128)S(1)}, u32[]{:S(2)}, u32[]{:S(2)}) collective-permute-start(f32[4,32,320]{2,1,0:T(8,128)S(1)} %get-tuple-element.9), channel_id=1, source_target_pairs={{0,16},{1,17},{2,18},{3,19},{4,20},{5,21},{6,22},{7,23},{8,24},{9,... | collective-permute-start | bytes 491528 | tf_op jit(solution)/shard_map/ppermute | solution.py:20
  169.7 16.8 %collective-permute-start.21 = (f32[4,32,320]{2,1,0:T(8,128)S(1)}, f32[4,32,320]{2,1,0:T(8,128)S(1)}, u32[]{:S(2)}, u32[]{:S(2)}) collective-permute-start(f32[4,32,320]{2,1,0:T(8,128)S(1)} %get-tuple-element.10), channel_id=1, source_target_pairs={{0,8},{1,9},{2,10},{3,11},{4,12},{5,13},{6,14},{7,15},{8,16},{9,17... | collective-permute-start | bytes 491528 | tf_op jit(solution)/shard_map/ppermute | solution.py:20
  181.1 8.3 %collective-permute-start.22 = (f32[4,32,320]{2,1,0:T(8,128)S(1)}, f32[4,32,320]{2,1,0:T(8,128)S(1)}, u32[]{:S(2)}, u32[]{:S(2)}) collective-permute-start(f32[4,32,320]{2,1,0:T(8,128)S(1)} %get-tuple-element.10), channel_id=1, source_target_pairs={{0,24},{1,25},{2,26},{3,27},{4,28},{5,29},{6,30},{7,31},{8,0},{9,1... | collective-permute-start | bytes 491528 | tf_op jit(solution)/shard_map/ppermute | solution.py:20
  189.4 19.4 %collective-permute-start.23 = (f32[32,320]{1,0:T(8,128)S(1)}, f32[32,320]{1,0:T(8,128)S(1)}, u32[]{:S(2)}, u32[]{:S(2)}) collective-permute-start(f32[32,320]{1,0:T(8,128)S(1)} %get-tuple-element.15), channel_id=1, source_target_pairs={{0,2},{1,3},{2,4},{3,5},{4,6},{5,7},{6,0},{7,1},{8,10},{9,11},{10,... | collective-permute-start | bytes 122888 | tf_op jit(solution)/shard_map/ppermute | solution.py:25
  191.4 17.6 %collective-permute-start.24 = (f32[32,320]{1,0:T(8,128)S(1)}, f32[32,320]{1,0:T(8,128)S(1)}, u32[]{:S(2)}, u32[]{:S(2)}) collective-permute-start(f32[32,320]{1,0:T(8,128)S(1)} %get-tuple-element.17), channel_id=1, source_target_pairs={{0,4},{1,5},{2,6},{3,7},{4,0},{5,1},{6,2},{7,3},{8,12},{9,13},{10,... | collective-permute-start | bytes 122888 | tf_op jit(solution)/shard_map/ppermute | solution.py:25
  (4 other events, 47.6 us)

commit v2 on v1

v2 whole, which is shorter than its diff:
```python
import jax
import jax.numpy as jnp
from jax import lax
from jax.sharding import PartitionSpec as P

FIRST = (0, 8, 1, 9)
HIGH = lax.Precision.HIGH
HIGHEST = lax.Precision.HIGHEST


def move_z(value, step):
    return lax.ppermute(value, "vr", [(4 * z + y, 4 * ((z + step) % 4) + y) for z in range(4) for y in range(4)])


def move_y(value, step):
    return lax.ppermute(value, "vr", [(4 * z + y, 4 * z + (y + step) % 4) for z in range(4) for y in range(4)])


def move_x(value, step):
    return lax.ppermute(value, "vc", [(8 * x + r, 8 * ((x + step) % 4) + r) for x in range(4) for r in range(8)])


def move_low(value, step):
    pairs = [(8 * x + 2 * k + c, 8 * x + 2 * ((k + step) % 4) + c) for x in range(4) for k in range(4) for c in range(2)]
    return lax.ppermute(value, "vc", pairs)


def move_core(value):
    return lax.ppermute(value, "vc", [(c, c ^ 1) for c in range(32)])


def slots_of_my_block(mirror_slot):
    pairs = []
    for z in range(4):
        for y in range(4):
            block = FIRST[z] + 2 * y
            for i in range(16):
                pairs.append((32 * i + block, 32 * (4 * z + y) + i))
                pairs.append((32 * i + block + 16, 32 * (4 * z + y) + i + 16))
    return lax.ppermute(mirror_slot, ("vr", "vc"), pairs)


SAME_CORE = [[8 * x + 2 * k + c for x in range(4) for k in range(4)] for c in range(2)]
SAME_PAIR = [[8 * x + 2 * k + c for x in (p, p + 1) for k in range(4)] for p in (0, 2) for c in range(2)]
SAME_Z = [[4 * z + y for y in range(4)] for z in range(4)]


SAME_Y = [[4 * z + y for z in range(4)] for y in range(4)]


def all_y(value):
    copies = jnp.broadcast_to(value[None], (4,) + value.shape)
    return lax.all_to_all(copies, "vr", 0, 0, axis_index_groups=SAME_Z)


def all_y_gather(value):
    return lax.all_gather(value, "vr", axis=0, axis_index_groups=SAME_Z)


def all_z(value):
    return lax.all_gather(value, "vr", axis=0, axis_index_groups=SAME_Y)


def local(amplitudes, integrals, mirror_slot):
    vr, vc = lax.axis_index("vr"), lax.axis_index("vc")
    z = vr // 4
    x, core = vc // 8, vc % 2
    iota = jnp.arange(32, dtype=jnp.int32)
    low_half = z < 2

    half = 32 * (z // 2)
    kept = lax.dynamic_slice_in_dim(amplitudes, half, 32, 0)
    other = move_z(lax.dynamic_slice_in_dim(amplitudes, 32 - half, 32, 0), 2)
    slots = slots_of_my_block(mirror_slot)
    chosen = jnp.where(vc < 16, slots[:, None] == iota[None, :], slots[None, :] == iota[:, None])
    first, second = jnp.where(low_half, kept, other), jnp.where(low_half, other, kept)
    mine = first - jnp.dot(chosen.astype(jnp.float32), second, precision=HIGHEST)

    def product(value):
        rows = value.shape[1]
        value = lax.dot_general(value.reshape(4 * rows, -1), integrals, (((1,), (1,)), ((), ())), precision=HIGH, preferred_element_type=jnp.float32)
        return value.reshape(4, rows, 320)

    def others(value):
        return jnp.concatenate([lax.dynamic_index_in_dim(value, (z + d) % 4, 0, False) for d in (1, 2, 3)], 0)

    own = all_y(mine)
    upper = all_z(mine[:16])
    lower, own = lax.optimization_barrier((mine[16:], own))
    upper = all_y(others(upper))
    lower = all_z(lower)
    lower, upper = lax.optimization_barrier((lower, upper))
    lower = all_y(others(lower))

    own, upper = lax.optimization_barrier((product(own), product(upper)))
    lower = product(lower)
    above, far, below = [jnp.concatenate([upper[:, 16 * d : 16 * d + 16], lower[:, 16 * d : 16 * d + 16]], 1) for d in range(3)]

    own_core = (z >= 2) == (core == 1)
    above_core = ((z == 1) | (z == 2)) == (core == 1)
    pick = lambda test, a, b: (jnp.where(test, a, b), jnp.where(test, b, a))
    kept, given = pick(own_core, own, far)
    kept2, given2 = pick(above_core, above, below)
    total = jnp.stack([kept, kept2]) + move_core(jnp.stack([given, given2]))
    total = jnp.where(z % 2 == 1, total[::-1], total)
    total = jnp.sum(lax.all_to_all(total.reshape(8, 32, 320), "vc", 0, 0, axis_index_groups=SAME_PAIR), 0)
    total = total + move_x(total, 2)

    slot = jnp.where(vc < 16, iota, mirror_slot)
    signed = jnp.where(slot[:, None] == iota[None, :], jnp.where(vc < 16, 1.0, -1.0), 0.0)
    return jnp.dot(signed, total, precision=HIGHEST).T


def solution(mesh):
    in_specs = (P("vr", "vc"), P("vr", "vc"), P("vc"))
    out_specs = P("vr", "vc")
    return jax.shard_map(local, mesh=mesh, in_specs=in_specs, out_specs=out_specs, check_vma=False)
```

time: 216 us -> 203 us (0.940)
  the two profiles are of different devices: /device:TPU:352 before, /device:TPU:4 now
where the time goes in v2:
time: 203 us; the launch traced here: 202 us
  blocking collectives  83.2 us (41%)
  starting transfers between devices  57.2 us (28%)
  waiting for transfers between devices  39.7 us (20%)
  matrix products  15.6 us (8%)
  local copies, waits for them, and re-layouts  6.04 us (3%)
    all_gather x2, blocking collectives, all_z(): return lax.all_gather(value, 'vr', axis=0, axis_index_groups=SAME_Y)  51.9 us
    all_to_all x3, starting transfers between devices, all_y(): return lax.all_to_all(copies, 'vr', 0, 0, axis_index_groups=SAME_Z)  35.3 us
    all_to_all x1, blocking collectives, local(): lax.all_to_all(total.reshape(8, 32, 320), 'vc', 0, 0, axis_index_groups=S...  31.3 us
    all_to_all x3, waiting for transfers between devices, all_y(): return lax.all_to_all(copies, 'vr', 0, 0, axis_index_groups=SAME_Z)  20.8 us
    ppermute x1, starting transfers between devices, move_z(): lax.ppermute(value, 'vr', [(4 * z + y, 4 * ((z + step) % 4) + y) for z in...  15.7 us
    dot_general x3, matrix products, product(): lax.dot_general(value.reshape(4 * rows, -1), integrals, (((1,), (1,)), ((...  13.2 us
    ppermute x1, waiting for transfers between devices, move_z(): lax.ppermute(value, 'vr', [(4 * z + y, 4 * ((z + step) % 4) + y) for z in...  12.7 us
    broadcast_in_dim x3, local copies, waits for them, and re-layouts, all_y(): copies = jnp.broadcast_to(value[None], (4,) + value.shape)  4.66 us
  transfers between devices with their start and end apart: 7, of which 5 were waited for; matrix products, arithmetic and copies ran while one was open for 4% of the time, Pallas kernels for 0%

profile of v2, /device:TPU:4, one launch (start us, length us, event | category | flops | bytes accessed | tf_op | source)
XLA Modules:
  0.0 202.3 jit_solution(10743142479813502232)
XLA Ops:
  0.0 1.0 constant_dynamic-slice_fusion
  1.0 15.7 %collective-permute-start = (f32[32,3200]{1,0:T(8,128)S(1)}, f32[32,3200]{1,0:T(8,128)S(1)}, u32[]{:S(2)}, u32[]{:S(2)}) collective-permute-start(f32[32,3200]{1,0:T(8,128)S(1)} %constant_dynamic-slice_fusion), channel_id=1, source_target_pairs={{0,256},{32,288},{64,320},{96,352},{128,384},{160,416},{192,448},{... | collective-permute-start | bytes 1228808 | tf_op jit(solution)/shard_map/ppermute | solution.py:12
  16.8 1.3 collective-permute-start.1
  18.1 12.7 %collective-permute-done = f32[32,3200]{1,0:T(8,128)S(1)} collective-permute-done((f32[32,3200]{1,0:T(8,128)S(1)}, f32[32,3200]{1,0:T(8,128)S(1)}, u32[]{:S(2)}, u32[]{:S(2)}) %collective-permute-start) | collective-permute-done | bytes 409632 | tf_op jit(solution)/shard_map/ppermute | solution.py:12
  30.8 1.5 select_subtract_fusion
  32.3 1.3 broadcast_in_dim.12
  33.6 26.5 %all-to-all-start = ((f32[4,32,3200]{2,1,0:T(8,128)}), f32[4,32,3200]{2,1,0:T(8,128)S(1)}, u32[]{:S(2)}, u32[]{:S(2)}) async-start(f32[4,32,3200]{2,1,0:T(8,128)} %broadcast_in_dim.12), calls=%async_computation | async-start | bytes 3276800 | tf_op jit(solution)/shard_map/all_to_all | solution.py:53
  60.1 25.8 %all-gather.1 = f32[64,3200]{1,0:T(8,128)S(1)} all-gather(f32[16,3200]{1,0:T(8,128)S(1)} %get-tuple-element.23), channel_id=3, replica_groups={{0,128,256,384},{32,160,288,416},{64,192,320,448},{96,224,352,480},{1,1..., dimensions={0}, use_global_device_ids=true | all-gather | bytes 1024000 | tf_op jit(solution)/shard_map/all_gather | solution.py:61
  86.0 1.7 broadcast_in_dim.13
  87.9 4.3 %all-to-all-start.1 = ((f32[4,48,3200]{2,1,0:T(8,128)}), f32[4,48,3200]{2,1,0:T(8,128)S(1)}, u32[]{:S(2)}, u32[]{:S(2)}) async-start(f32[4,48,3200]{2,1,0:T(8,128)} %broadcast_in_dim.13), calls=%async_computation.1 | async-start | bytes 4915200 | tf_op jit(solution)/shard_map/all_to_all | solution.py:53
  92.2 26.1 %all-gather = f32[64,3200]{1,0:T(8,128)S(1)} all-gather(f32[16,3200]{1,0:T(8,128)S(1)} %get-tuple-element.12), channel_id=2, replica_groups={{0,128,256,384},{32,160,288,416},{64,192,320,448},{96,224,352,480},{1,1..., dimensions={0}, use_global_device_ids=true | all-gather | bytes 1024000 | tf_op jit(solution)/shard_map/all_gather | solution.py:61
  118.3 1.8 all-to-all-done.1
  120.2 1.6 broadcast_in_dim.14
  121.8 4.5 %all-to-all-start.2 = ((f32[4,48,3200]{2,1,0:T(8,128)}), f32[4,48,3200]{2,1,0:T(8,128)}, u32[]{:S(2)}, u32[]{:S(2)}) async-start(f32[4,48,3200]{2,1,0:T(8,128)} %broadcast_in_dim.14), calls=%async_computation.2 | async-start | bytes 4915200 | tf_op jit(solution)/shard_map/all_to_all | solution.py:53
  126.4 5.1 %fusion.4 = f32[4,32,320]{2,1,0:T(8,128)S(1)} fusion(f32[4,32,3200]{2,1,0:T(8,128)} %copy-done.1, f32[320,3200]{1,0:T(8,128)} %param.4), kind=kOutput, calls=%fused_computation.4 | convolution fusion | flops 786432000 | bytes 5898240 | tf_op jit(solution)/shard_map/dot_general | solution.py:81
  131.5 2.7 %fusion.2 = f32[4,48,320]{2,1,0:T(8,128)S(1)} fusion(f32[4,48,3200]{2,1,0:T(8,128)S(1)} %all-to-all-done.1, f32[320,3200]{1,0:T(8,128)S(1)} %copy-done), kind=kOutput, calls=%fused_computation.2 | convolution fusion | flops 1179648000 | bytes 6799360 | tf_op jit(solution)/shard_map/dot_general | solution.py:81
  134.2 19.1 %all-to-all-done.2 = f32[4,48,3200]{2,1,0:T(8,128)} async-done(((f32[4,48,3200]{2,1,0:T(8,128)}), f32[4,48,3200]{2,1,0:T(8,128)}, u32[]{:S(2)}, u32[]{:S(2)}) %all-to-all-start.2) | async-done | bytes 2457632 | tf_op jit(solution)/shard_map/all_to_all | solution.py:53
  153.3 5.4 %fusion = f32[4,48,320]{2,1,0:T(8,128)S(1)} fusion(f32[4,48,3200]{2,1,0:T(8,128)} %all-to-all-done.2, f32[320,3200]{1,0:T(8,128)} %param.4), kind=kOutput, calls=%fused_computation | convolution fusion | flops 1179648000 | bytes 6799360 | tf_op jit(solution)/shard_map/dot_general | solution.py:81
  158.9 1.9 collective-permute-start.2
  160.8 1.7 collective-permute-done.2
  162.6 31.3 %all_to_all.20 = f32[8,32,320]{2,1,0:T(8,128)S(1)} all-to-all(f32[8,32,320]{2,1,0:T(8,128)S(1)} %bitcast.39), channel_id=1, replica_groups={{0,2,4,6,8,10,12,14},{1,3,5,7,9,11,13,15},{16,18,20,22,24,26,28,30},{17..., dimensions={0} | all-to-all | bytes 655360 | tf_op jit(solution)/shard_map/all_to_all | solution.py:106
  193.9 3.0 %collective-permute-start.3 = (f32[32,320]{1,0:T(8,128)S(1)}, f32[32,320]{1,0:T(8,128)S(1)}, u32[]{:S(2)}, u32[]{:S(2)}) collective-permute-start(f32[32,320]{1,0:T(8,128)S(1)} %reduce_sum.9), channel_id=1, source_target_pairs={{0,16},{1,17},{2,18},{3,19},{4,20},{5,21},{6,22},{7,23},{8,24},{9,... | collective-permute-start | bytes 122888 | tf_op jit(solution)/shard_map/ppermute | solution.py:20
  197.0 4.5 %collective-permute-done.3 = f32[32,320]{1,0:T(8,128)S(1)} collective-permute-done((f32[32,320]{1,0:T(8,128)S(1)}, f32[32,320]{1,0:T(8,128)S(1)}, u32[]{:S(2)}, u32[]{:S(2)}) %collective-permute-start.3) | collective-permute-done | bytes 40992 | tf_op jit(solution)/shard_map/ppermute | solution.py:20
  201.4 0.9 fusion.14
  (22 shorter events, 0.7 us)
Async XLA Ops:
  1.0 29.7 %collective-permute-start = (f32[32,3200]{1,0:T(8,128)S(1)}, f32[32,3200]{1,0:T(8,128)S(1)}, u32[]{:S(2)}, u32[]{:S(2)}) collective-permute-start(f32[32,3200]{1,0:T(8,128)S(1)} %constant_dynamic-slice_fusion), channel_id=1, source_target_pairs={{0,256},{32,288},{64,320},{96,352},{128,384},{160,416},{192,448},{... | collective-permute-start | bytes 1228808 | tf_op jit(solution)/shard_map/ppermute | solution.py:12
  16.8 1.3 collective-permute-start.1
  33.6 52.3 %all-to-all-start = ((f32[4,32,3200]{2,1,0:T(8,128)}), f32[4,32,3200]{2,1,0:T(8,128)S(1)}, u32[]{:S(2)}, u32[]{:S(2)}) async-start(f32[4,32,3200]{2,1,0:T(8,128)} %broadcast_in_dim.12), calls=%async_computation | async-start | bytes 3276800 | tf_op jit(solution)/shard_map/all_to_all | solution.py:53
  86.0 1.9 copy-start.1
  87.9 32.2 %all-to-all-start.1 = ((f32[4,48,3200]{2,1,0:T(8,128)}), f32[4,48,3200]{2,1,0:T(8,128)S(1)}, u32[]{:S(2)}, u32[]{:S(2)}) async-start(f32[4,48,3200]{2,1,0:T(8,128)} %broadcast_in_dim.13), calls=%async_computation.1 | async-start | bytes 4915200 | tf_op jit(solution)/shard_map/all_to_all | solution.py:53
  121.8 31.5 %all-to-all-start.2 = ((f32[4,48,3200]{2,1,0:T(8,128)}), f32[4,48,3200]{2,1,0:T(8,128)}, u32[]{:S(2)}, u32[]{:S(2)}) async-start(f32[4,48,3200]{2,1,0:T(8,128)} %broadcast_in_dim.14), calls=%async_computation.2 | async-start | bytes 4915200 | tf_op jit(solution)/shard_map/all_to_all | solution.py:53
  126.3 5.1 %copy-start = (f32[320,3200]{1,0:T(8,128)S(1)}, f32[320,3200]{1,0:T(8,128)}, u32[]{:S(2)}) copy-start(f32[320,3200]{1,0:T(8,128)} %param.4) | copy-start | bytes 12288004
  158.8 38.1 %copy-start.2 = (s32[32]{0:T(128)S(1)}, s32[32]{0:T(128)}, u32[]{:S(2)}) copy-start(s32[32]{0:T(128)} %param.5) | copy-start | bytes 388
  158.9 3.6 %collective-permute-start.2 = (f32[2,4,32,320]{3,2,1,0:T(8,128)S(1)}, f32[2,4,32,320]{3,2,1,0:T(8,128)S(1)}, u32[]{:S(2)}, u32[]{:S(2)}) collective-permute-start(f32[2,4,32,320]{3,2,1,0:T(8,128)S(1)} %pad_maximum_fusion.2), channel_id=1, source_target_pairs={{0,1},{1,0},{2,3},{3,2},{4,5},{5,4},{6,7},{7,6},{8,9},{9,8},{10,11... | collective-permute-start | bytes 983048 | tf_op jit(solution)/shard_map/ppermute | solution.py:29
  193.9 7.5 %collective-permute-start.3 = (f32[32,320]{1,0:T(8,128)S(1)}, f32[32,320]{1,0:T(8,128)S(1)}, u32[]{:S(2)}, u32[]{:S(2)}) collective-permute-start(f32[32,320]{1,0:T(8,128)S(1)} %reduce_sum.9), channel_id=1, source_target_pairs={{0,16},{1,17},{2,18},{3,19},{4,20},{5,21},{6,22},{7,23},{8,24},{9,... | collective-permute-start | bytes 122888 | tf_op jit(solution)/shard_map/ppermute | solution.py:20

commit v3 on v2

--- a/solution.py
+++ b/solution.py
@@ -78,8 +78,9 @@
 
     def product(value):
         rows = value.shape[1]
-        value = lax.dot_general(value.reshape(4 * rows, -1), integrals, (((1,), (1,)), ((), ())), precision=HIGH, preferred_element_type=jnp.float32)
-        return value.reshape(4, rows, 320)
+        count = value.shape[0]
+        value = lax.dot_general(value.reshape(count * rows, -1), integrals, (((1,), (1,)), ((), ())), precision=HIGH, preferred_element_type=jnp.float32)
+        return value.reshape(count, rows, 320)
 
     def others(value):
         return jnp.concatenate([lax.dynamic_index_in_dim(value, (z + d) % 4, 0, False) for d in (1, 2, 3)], 0)
@@ -90,10 +91,15 @@
     upper = all_y(others(upper))
     lower = all_z(lower)
     lower, upper = lax.optimization_barrier((lower, upper))
-    lower = all_y(others(lower))
+    lower = others(lower)
+    last_y, next_y = move_y(lower, 1), move_y(lower, 3)
+    far_y = jnp.concatenate([move_y(last_y[:24], 1), move_y(next_y[24:], 3)], 0)
 
     own, upper = lax.optimization_barrier((product(own), product(upper)))
-    lower = product(lower)
+    lower = product(jnp.stack([lower, next_y, last_y]))
+    far_y = product(far_y[None])
+    lower = jnp.stack([lower[0], lower[1], far_y[0], lower[2]])
+    lower = lax.dynamic_slice_in_dim(jnp.concatenate([lower, lower], 0), (4 - vr % 4) % 4, 4, 0)
     above, far, below = [jnp.concatenate([upper[:, 16 * d : 16 * d + 16], lower[:, 16 * d : 16 * d + 16]], 1) for d in range(3)]
 
     own_core = (z >= 2) == (core == 1)

time: 203 us -> 196 us (0.966)
  the two profiles are of different devices: /device:TPU:4 before, /device:TPU:2 now
where the time goes in v3:
time: 196 us; the launch traced here: 195 us
  blocking collectives  93.2 us (48%)
  starting transfers between devices  59.5 us (30%)
  waiting for transfers between devices  23 us (12%)
  matrix products  14 us (7%)
  local copies, waits for them, and re-layouts  4.55 us (2%)
    all_gather x2, blocking collectives, all_z(): return lax.all_gather(value, 'vr', axis=0, axis_index_groups=SAME_Y)  74.1 us
    all_to_all x1, blocking collectives, local(): lax.all_to_all(total.reshape(8, 32, 320), 'vc', 0, 0, axis_index_groups=S...  19.1 us
    ppermute x4, starting transfers between devices, move_y(): lax.ppermute(value, 'vr', [(4 * z + y, 4 * z + (y + step) % 4) for z in r...  17.5 us
    all_to_all x2, starting transfers between devices, all_y(): return lax.all_to_all(copies, 'vr', 0, 0, axis_index_groups=SAME_Z)  17.5 us
    ppermute x1, starting transfers between devices, move_z(): lax.ppermute(value, 'vr', [(4 * z + y, 4 * ((z + step) % 4) + y) for z in...  15.7 us
    dot_general x4, matrix products, product(): lax.dot_general(value.reshape(count * rows, -1), integrals, (((1,), (1,))...  11.6 us
    ppermute x1, waiting for transfers between devices, slots_of_my_block(): return lax.ppermute(mirror_slot, ('vr', 'vc'), pairs)  11.1 us
    ppermute x4, waiting for transfers between devices, move_y(): lax.ppermute(value, 'vr', [(4 * z + y, 4 * z + (y + step) % 4) for z in r...  5.46 us
  transfers between devices with their start and end apart: 10, of which 4 were waited for; matrix products, arithmetic and copies ran while one was open for 5% of the time, Pallas kernels for 0%

profile of v3, /device:TPU:2, one launch (start us, length us, event | category | flops | bytes accessed | tf_op | source)
XLA Modules:
  0.0 195.1 jit_solution(1792984891420251538)
XLA Ops:
  1.0 15.7 %collective-permute-start = (f32[32,3200]{1,0:T(8,128)S(1)}, f32[32,3200]{1,0:T(8,128)S(1)}, u32[]{:S(2)}, u32[]{:S(2)}) collective-permute-start(f32[32,3200]{1,0:T(8,128)S(1)} %constant_dynamic-slice_fusion.1), channel_id=1, source_target_pairs={{0,256},{32,288},{64,320},{96,352},{128,384},{160,416},{192,448},{... | collective-permute-start | bytes 1228808 | tf_op jit(solution)/shard_map/ppermute | solution.py:12
  16.8 4.3 %collective-permute-start.1 = (s32[32]{0:T(128)}, s32[32]{0:T(128)S(1)}, u32[]{:S(2)}, u32[]{:S(2)}) collective-permute-start(s32[32]{0:T(128)} %param.5), channel_id=1, source_target_pairs={{0,0},{16,16},{32,1},{48,17},{64,2},{80,18},{96,3},{112,19},{128,4... | collective-permute-start | bytes 392 | tf_op jit(solution)/shard_map/ppermute | solution.py:40
  21.1 11.1 %collective-permute-done.1 = s32[32]{0:T(128)S(1)} collective-permute-done((s32[32]{0:T(128)}, s32[32]{0:T(128)S(1)}, u32[]{:S(2)}, u32[]{:S(2)}) %collective-permute-start.1) | collective-permute-done | bytes 160 | tf_op jit(solution)/shard_map/ppermute | solution.py:40
  32.2 1.5 select_subtract_fusion
  33.7 1.3 broadcast_in_dim.10
  35.0 13.0 %all-to-all-start = ((f32[4,32,3200]{2,1,0:T(8,128)}), f32[4,32,3200]{2,1,0:T(8,128)S(1)}, u32[]{:S(2)}, u32[]{:S(2)}) async-start(f32[4,32,3200]{2,1,0:T(8,128)} %broadcast_in_dim.10), calls=%async_computation | async-start | bytes 3276800 | tf_op jit(solution)/shard_map/all_to_all | solution.py:53
  48.1 36.8 %all-gather.1 = f32[64,3200]{1,0:T(8,128)S(1)} all-gather(f32[16,3200]{1,0:T(8,128)S(1)} %get-tuple-element.28), channel_id=3, replica_groups={{0,128,256,384},{32,160,288,416},{64,192,320,448},{96,224,352,480},{1,1..., dimensions={0}, use_global_device_ids=true | all-gather | bytes 1024000 | tf_op jit(solution)/shard_map/all_gather | solution.py:61
  85.0 1.7 broadcast_in_dim.11
  86.9 4.4 %all-to-all-start.1 = ((f32[4,48,3200]{2,1,0:T(8,128)}), f32[4,48,3200]{2,1,0:T(8,128)S(1)}, u32[]{:S(2)}, u32[]{:S(2)}) async-start(f32[4,48,3200]{2,1,0:T(8,128)} %broadcast_in_dim.11), calls=%async_computation.1 | async-start | bytes 4915200 | tf_op jit(solution)/shard_map/all_to_all | solution.py:53
  91.4 37.3 %all-gather = f32[64,3200]{1,0:T(8,128)S(1)} all-gather(f32[16,3200]{1,0:T(8,128)S(1)} %get-tuple-element.12), channel_id=2, replica_groups={{0,128,256,384},{32,160,288,416},{64,192,320,448},{96,224,352,480},{1,1..., dimensions={0}, use_global_device_ids=true | all-gather | bytes 1024000 | tf_op jit(solution)/shard_map/all_gather | solution.py:61
  128.9 8.5 %collective-permute-start.2 = (f32[48,3200]{1,0:T(8,128)S(1)}, f32[48,3200]{1,0:T(8,128)S(1)}, u32[]{:S(2)}, u32[]{:S(2)}) collective-permute-start(f32[48,3200]{1,0:T(8,128)S(1)} %get-tuple-element.24), channel_id=1, source_target_pairs={{0,96},{32,0},{64,32},{96,64},{128,224},{160,128},{192,160},{224,1... | collective-permute-start | bytes 1843208 | tf_op jit(solution)/shard_map/ppermute | solution.py:16
  137.4 1.9 collective-permute-start.3
  139.3 4.5 %fusion.2 = f32[4,32,320]{2,1,0:T(8,128)S(1)} fusion(f32[4,32,3200]{2,1,0:T(8,128)S(1)} %copy-done.2, f32[320,3200]{1,0:T(8,128)} %param.4), kind=kOutput, calls=%fused_computation.2 | convolution fusion | flops 786432000 | bytes 5898240 | tf_op jit(solution)/shard_map/dot_general | solution.py:82
  143.8 2.7 %fusion = f32[4,48,320]{2,1,0:T(8,128)S(1)} fusion(f32[4,48,3200]{2,1,0:T(8,128)S(1)} %all-to-all-done.1, f32[320,3200]{1,0:T(8,128)S(1)} %copy-done), kind=kOutput, calls=%fused_computation | convolution fusion | flops 1179648000 | bytes 6799360 | tf_op jit(solution)/shard_map/dot_general | solution.py:82
  146.6 5.1 %collective-permute-start.5 = (f32[24,3200]{1,0:T(8,128)S(1)}, f32[24,3200]{1,0:T(8,128)S(1)}, u32[]{:S(2)}, u32[]{:S(2)}) collective-permute-start(f32[24,3200]{1,0:T(8,128)S(1)} %slice.69), channel_id=1, source_target_pairs={{0,96},{32,0},{64,32},{96,64},{128,224},{160,128},{192,160},{224,1... | collective-permute-start | bytes 921608 | tf_op jit(solution)/shard_map/ppermute | solution.py:16
  151.7 1.9 collective-permute-start.4
  153.8 2.4 %fusion.38 = f32[144,320]{1,0:T(8,128)S(1)} fusion(f32[144,3200]{1,0:T(8,128)S(1)} %bitcast.62, f32[320,3200]{1,0:T(8,128)S(1)} %copy-done), kind=kOutput, calls=%fused_computation.69 | convolution fusion | flops 884736000 | bytes 6123520 | tf_op jit(solution)/shard_map/dot_general | solution.py:82
  156.2 5.4 %collective-permute-done.4 = f32[24,3200]{1,0:T(8,128)S(1)} collective-permute-done((f32[24,3200]{1,0:T(8,128)S(1)}, f32[24,3200]{1,0:T(8,128)S(1)}, u32[]{:S(2)}, u32[]{:S(2)}) %collective-permute-start.4) | collective-permute-done | bytes 307232 | tf_op jit(solution)/shard_map/ppermute | solution.py:16
  161.7 2.0 %constant_dynamic-update-slice_fusion.1 = (f32[8,48,320]{2,1,0:T(8,128)S(1)}, f32[1,48,320]{2,1,0:T(8,128)S(1)}) fusion(f32[8,48,320]{2,1,0:T(8,128)S(1)} %fusion.17, f32[320,3200]{1,0:T(8,128)S(1)} %copy-done, f32[24,3200]{1,0:T(8,128)S(1)} %collective-permute-done.5, f32[24,3200]{1,0:T(8,128)S(1)} %collective-permute-done.4), kind=kOutput, calls=%fused_computation.48 | convolution fusion | flops 295065600 | bytes 4857856 | tf_op jit(solution)/shard_map/dot_general | solution.py:82
  164.0 1.9 collective-permute-start.6
  165.9 1.7 collective-permute-done.6
  167.7 19.1 %all_to_all.15 = f32[8,32,320]{2,1,0:T(8,128)S(1)} all-to-all(f32[8,32,320]{2,1,0:T(8,128)S(1)} %bitcast.65), channel_id=1, replica_groups={{0,2,4,6,8,10,12,14},{1,3,5,7,9,11,13,15},{16,18,20,22,24,26,28,30},{17..., dimensions={0} | all-to-all | bytes 655360 | tf_op jit(solution)/shard_map/all_to_all | solution.py:112
  186.8 2.7 %collective-permute-start.7 = (f32[32,320]{1,0:T(8,128)S(1)}, f32[32,320]{1,0:T(8,128)S(1)}, u32[]{:S(2)}, u32[]{:S(2)}) collective-permute-start(f32[32,320]{1,0:T(8,128)S(1)} %reduce_sum.9), channel_id=1, source_target_pairs={{0,16},{1,17},{2,18},{3,19},{4,20},{5,21},{6,22},{7,23},{8,24},{9,... | collective-permute-start | bytes 122888 | tf_op jit(solution)/shard_map/ppermute | solution.py:20
  189.5 4.8 %collective-permute-done.7 = f32[32,320]{1,0:T(8,128)S(1)} collective-permute-done((f32[32,320]{1,0:T(8,128)S(1)}, f32[32,320]{1,0:T(8,128)S(1)}, u32[]{:S(2)}, u32[]{:S(2)}) %collective-permute-start.7) | collective-permute-done | bytes 40992 | tf_op jit(solution)/shard_map/ppermute | solution.py:20
  (39 shorter events, 2.9 us)
Async XLA Ops:
  1.0 31.1 %collective-permute-start = (f32[32,3200]{1,0:T(8,128)S(1)}, f32[32,3200]{1,0:T(8,128)S(1)}, u32[]{:S(2)}, u32[]{:S(2)}) collective-permute-start(f32[32,3200]{1,0:T(8,128)S(1)} %constant_dynamic-slice_fusion.1), channel_id=1, source_target_pairs={{0,256},{32,288},{64,320},{96,352},{128,384},{160,416},{192,448},{... | collective-permute-start | bytes 1228808 | tf_op jit(solution)/shard_map/ppermute | solution.py:12
  16.8 15.4 %collective-permute-start.1 = (s32[32]{0:T(128)}, s32[32]{0:T(128)S(1)}, u32[]{:S(2)}, u32[]{:S(2)}) collective-permute-start(s32[32]{0:T(128)} %param.5), channel_id=1, source_target_pairs={{0,0},{16,16},{32,1},{48,17},{64,2},{80,18},{96,3},{112,19},{128,4... | collective-permute-start | bytes 392 | tf_op jit(solution)/shard_map/ppermute | solution.py:40
  35.0 50.0 %all-to-all-start = ((f32[4,32,3200]{2,1,0:T(8,128)}), f32[4,32,3200]{2,1,0:T(8,128)S(1)}, u32[]{:S(2)}, u32[]{:S(2)}) async-start(f32[4,32,3200]{2,1,0:T(8,128)} %broadcast_in_dim.10), calls=%async_computation | async-start | bytes 3276800 | tf_op jit(solution)/shard_map/all_to_all | solution.py:53
  85.0 2.0 %copy-start.1 = (f32[4,32,3200]{2,1,0:T(8,128)}, f32[4,32,3200]{2,1,0:T(8,128)S(1)}, u32[]{:S(2)}) copy-start(f32[4,32,3200]{2,1,0:T(8,128)S(1)} %all-to-all-done) | copy-start | bytes 4915204
  86.9 41.8 %all-to-all-start.1 = ((f32[4,48,3200]{2,1,0:T(8,128)}), f32[4,48,3200]{2,1,0:T(8,128)S(1)}, u32[]{:S(2)}, u32[]{:S(2)}) async-start(f32[4,48,3200]{2,1,0:T(8,128)} %broadcast_in_dim.11), calls=%async_computation.1 | async-start | bytes 4915200 | tf_op jit(solution)/shard_map/all_to_all | solution.py:53
  128.7 10.6 %copy-start.2 = (f32[4,32,3200]{2,1,0:T(8,128)S(1)}, f32[4,32,3200]{2,1,0:T(8,128)}, u32[]{:S(2)}) copy-start(f32[4,32,3200]{2,1,0:T(8,128)} %copy-done.1) | copy-start | bytes 4915204
  128.8 14.9 %copy-start = (f32[320,3200]{1,0:T(8,128)S(1)}, f32[320,3200]{1,0:T(8,128)}, u32[]{:S(2)}) copy-start(f32[320,3200]{1,0:T(8,128)} %param.4) | copy-start | bytes 12288004
  128.9 17.7 %collective-permute-start.2 = (f32[48,3200]{1,0:T(8,128)S(1)}, f32[48,3200]{1,0:T(8,128)S(1)}, u32[]{:S(2)}, u32[]{:S(2)}) collective-permute-start(f32[48,3200]{1,0:T(8,128)S(1)} %get-tuple-element.24), channel_id=1, source_target_pairs={{0,96},{32,0},{64,32},{96,64},{128,224},{160,128},{192,160},{224,1... | collective-permute-start | bytes 1843208 | tf_op jit(solution)/shard_map/ppermute | solution.py:16
  137.4 14.3 %collective-permute-start.3 = (f32[48,3200]{1,0:T(8,128)S(1)}, f32[48,3200]{1,0:T(8,128)S(1)}, u32[]{:S(2)}, u32[]{:S(2)}) collective-permute-start(f32[48,3200]{1,0:T(8,128)S(1)} %get-tuple-element.24), channel_id=1, source_target_pairs={{0,32},{32,64},{64,96},{96,0},{128,160},{160,192},{192,224},{224,1... | collective-permute-start | bytes 1843208 | tf_op jit(solution)/shard_map/ppermute | solution.py:16
  146.6 9.7 %collective-permute-start.5 = (f32[24,3200]{1,0:T(8,128)S(1)}, f32[24,3200]{1,0:T(8,128)S(1)}, u32[]{:S(2)}, u32[]{:S(2)}) collective-permute-start(f32[24,3200]{1,0:T(8,128)S(1)} %slice.69), channel_id=1, source_target_pairs={{0,96},{32,0},{64,32},{96,64},{128,224},{160,128},{192,160},{224,1... | collective-permute-start | bytes 921608 | tf_op jit(solution)/shard_map/ppermute | solution.py:16
  151.7 10.0 %collective-permute-start.4 = (f32[24,3200]{1,0:T(8,128)S(1)}, f32[24,3200]{1,0:T(8,128)S(1)}, u32[]{:S(2)}, u32[]{:S(2)}) collective-permute-start(f32[24,3200]{1,0:T(8,128)S(1)} %slice.68), channel_id=1, source_target_pairs={{0,32},{32,64},{64,96},{96,0},{128,160},{160,192},{192,224},{224,1... | collective-permute-start | bytes 921608 | tf_op jit(solution)/shard_map/ppermute | solution.py:16
  163.9 25.6 %copy-start.3 = (s32[32]{0:T(128)S(1)}, s32[32]{0:T(128)}, u32[]{:S(2)}) copy-start(s32[32]{0:T(128)} %param.5) | copy-start | bytes 388
  164.0 3.6 %collective-permute-start.6 = (f32[2,4,32,320]{3,2,1,0:T(8,128)S(1)}, f32[2,4,32,320]{3,2,1,0:T(8,128)S(1)}, u32[]{:S(2)}, u32[]{:S(2)}) collective-permute-start(f32[2,4,32,320]{3,2,1,0:T(8,128)S(1)} %pad_maximum_fusion.3), channel_id=1, source_target_pairs={{0,1},{1,0},{2,3},{3,2},{4,5},{5,4},{6,7},{7,6},{8,9},{9,8},{10,11... | collective-permute-start | bytes 983048 | tf_op jit(solution)/shard_map/ppermute | solution.py:29
  186.8 7.5 %collective-permute-start.7 = (f32[32,320]{1,0:T(8,128)S(1)}, f32[32,320]{1,0:T(8,128)S(1)}, u32[]{:S(2)}, u32[]{:S(2)}) collective-permute-start(f32[32,320]{1,0:T(8,128)S(1)} %reduce_sum.9), channel_id=1, source_target_pairs={{0,16},{1,17},{2,18},{3,19},{4,20},{5,21},{6,22},{7,23},{8,24},{9,... | collective-permute-start | bytes 122888 | tf_op jit(solution)/shard_map/ppermute | solution.py:20

commit v4 on v2

--- a/solution.py
+++ b/solution.py
@@ -4,6 +4,7 @@
 from jax.sharding import PartitionSpec as P
 
 FIRST = (0, 8, 1, 9)
+CUT = 1664
 HIGH = lax.Precision.HIGH
 HIGHEST = lax.Precision.HIGHEST
 
@@ -76,25 +77,31 @@
     first, second = jnp.where(low_half, kept, other), jnp.where(low_half, other, kept)
     mine = first - jnp.dot(chosen.astype(jnp.float32), second, precision=HIGHEST)
 
-    def product(value):
-        rows = value.shape[1]
-        value = lax.dot_general(value.reshape(4 * rows, -1), integrals, (((1,), (1,)), ((), ())), precision=HIGH, preferred_element_type=jnp.float32)
-        return value.reshape(4, rows, 320)
+    def product(value, integrals):
+        count, rows = value.shape[:2]
+        value = lax.dot_general(value.reshape(count * rows, -1), integrals, (((1,), (1,)), ((), ())), precision=HIGH, preferred_element_type=jnp.float32)
+        return value.reshape(count, rows, 320)
 
     def others(value):
         return jnp.concatenate([lax.dynamic_index_in_dim(value, (z + d) % 4, 0, False) for d in (1, 2, 3)], 0)
 
     own = all_y(mine)
-    upper = all_z(mine[:16])
-    lower, own = lax.optimization_barrier((mine[16:], own))
-    upper = all_y(others(upper))
-    lower = all_z(lower)
-    lower, upper = lax.optimization_barrier((lower, upper))
-    lower = all_y(others(lower))
+    early = all_z(mine[:, :CUT])
+    late, own = lax.optimization_barrier((mine[:, CUT:], own))
+    early = all_y(others(early))
+    late = all_z(late)
+    late, early = lax.optimization_barrier((late, early))
+    late = others(late)
+    last_y, next_y = move_y(late, 1), move_y(late, 3)
+    far_y = jnp.concatenate([move_y(last_y[:48], 1), move_y(next_y[48:], 3)], 0)
 
-    own, upper = lax.optimization_barrier((product(own), product(upper)))
-    lower = product(lower)
-    above, far, below = [jnp.concatenate([upper[:, 16 * d : 16 * d + 16], lower[:, 16 * d : 16 * d + 16]], 1) for d in range(3)]
+    own, early = lax.optimization_barrier((product(own, integrals), product(early, integrals[:, :CUT])))
+    late = product(jnp.stack([late, next_y, last_y]), integrals[:, CUT:])
+    far_y = product(far_y[None], integrals[:, CUT:])
+    late = jnp.stack([late[0], late[1], far_y[0], late[2]])
+    late = lax.dynamic_slice_in_dim(jnp.concatenate([late, late], 0), (4 - vr % 4) % 4, 4, 0)
+    total = early + late
+    above, far, below = total[:, :32], total[:, 32:64], total[:, 64:]
 
     own_core = (z >= 2) == (core == 1)
     above_core = ((z == 1) | (z == 2)) == (core == 1)

time: 203 us -> 196 us (0.966)
  waiting for transfers between devices: 39.7 us -> 25 us
  starting transfers between devices: 57.2 us -> 68.8 us
  matrix products: 15.6 us -> 11.8 us
    all_to_all x3 -> x2, waiting for transfers between devices: 20.8 us -> 0.93 us  [all_y(): return lax.all_to_all(copies, 'vr', 0, 0, axis_index_groups=SAME_Z)]
    ppermute x0 -> x4, starting transfers between devices: none -> 16.2 us  [move_y(): lax.ppermute(value, 'vr', [(4 * z + y, 4 * z + (y + step) % 4) for z in r...]
    ppermute x0 -> x4, waiting for transfers between devices: none -> 4.13 us  [move_y(): lax.ppermute(value, 'vr', [(4 * z + y, 4 * z + (y + step) % 4) for z in r...]
    dot_general x3 -> x4, matrix products: 13.2 us -> 9.46 us  [product(): lax.dot_general(value.reshape(count * rows, -1), integrals, (((1,), (1,))...]
    all_to_all x3 -> x2, starting transfers between devices: 35.3 us -> 31.7 us  [all_y(): return lax.all_to_all(copies, 'vr', 0, 0, axis_index_groups=SAME_Z)]
    broadcast_in_dim x3 -> x2, local copies, waits for them, and re-layouts: 4.66 us -> 3.05 us  [all_y(): copies = jnp.broadcast_to(value[None], (4,) + value.shape)]
  transfers between devices with their start and end apart: 7 -> 10, of which waited for: 5 -> 7; matrix products, arithmetic and copies ran while one was open for 4% -> 4% of each run, Pallas kernels for 0% -> 0%
where the time goes in v4:
time: 196 us; the launch traced here: 195 us
  blocking collectives  84.3 us (43%)
  starting transfers between devices  68.8 us (35%)
  waiting for transfers between devices  25 us (13%)
  matrix products  11.8 us (6%)
  local copies, waits for them, and re-layouts  4.55 us (2%)
    all_gather x2, blocking collectives, all_z(): return lax.all_gather(value, 'vr', axis=0, axis_index_groups=SAME_Y)  53 us
    all_to_all x2, starting transfers between devices, all_y(): return lax.all_to_all(copies, 'vr', 0, 0, axis_index_groups=SAME_Z)  31.7 us
    all_to_all x1, blocking collectives, local(): lax.all_to_all(total.reshape(8, 32, 320), 'vc', 0, 0, axis_index_groups=S...  31.3 us
    ppermute x4, starting transfers between devices, move_y(): lax.ppermute(value, 'vr', [(4 * z + y, 4 * z + (y + step) % 4) for z in r...  16.2 us
    ppermute x1, starting transfers between devices, move_z(): lax.ppermute(value, 'vr', [(4 * z + y, 4 * ((z + step) % 4) + y) for z in...  15.7 us
    ppermute x1, waiting for transfers between devices, move_z(): lax.ppermute(value, 'vr', [(4 * z + y, 4 * ((z + step) % 4) + y) for z in...  12.7 us
    dot_general x4, matrix products, product(): lax.dot_general(value.reshape(count * rows, -1), integrals, (((1,), (1,))...  9.46 us
    ppermute x1, waiting for transfers between devices, move_x(): lax.ppermute(value, 'vc', [(8 * x + r, 8 * ((x + step) % 4) + r) for x in...  5.53 us
  transfers between devices with their start and end apart: 10, of which 7 were waited for; matrix products, arithmetic and copies ran while one was open for 4% of the time, Pallas kernels for 0%

profile of v4, /device:TPU:4, one launch (start us, length us, event | category | flops | bytes accessed | tf_op | source)
XLA Modules:
  0.0 195.3 jit_solution(477748023661553106)
XLA Ops:
  1.0 15.7 %collective-permute-start = (f32[32,3200]{1,0:T(8,128)S(1)}, f32[32,3200]{1,0:T(8,128)S(1)}, u32[]{:S(2)}, u32[]{:S(2)}) collective-permute-start(f32[32,3200]{1,0:T(8,128)S(1)} %constant_dynamic-slice_fusion), channel_id=1, source_target_pairs={{0,256},{32,288},{64,320},{96,352},{128,384},{160,416},{192,448},{... | collective-permute-start | bytes 1228808 | tf_op jit(solution)/shard_map/ppermute | solution.py:13
  16.8 1.3 collective-permute-start.1
  18.1 12.7 %collective-permute-done = f32[32,3200]{1,0:T(8,128)S(1)} collective-permute-done((f32[32,3200]{1,0:T(8,128)S(1)}, f32[32,3200]{1,0:T(8,128)S(1)}, u32[]{:S(2)}, u32[]{:S(2)}) %collective-permute-start) | collective-permute-done | bytes 409632 | tf_op jit(solution)/shard_map/ppermute | solution.py:13
  30.8 1.5 select_subtract_fusion
  32.3 1.3 broadcast_in_dim.10
  33.6 26.5 %all-to-all-start = ((f32[4,32,3200]{2,1,0:T(8,128)}), f32[4,32,3200]{2,1,0:T(8,128)S(1)}, u32[]{:S(2)}, u32[]{:S(2)}) async-start(f32[4,32,3200]{2,1,0:T(8,128)} %broadcast_in_dim.10), calls=%async_computation | async-start | bytes 3276800 | tf_op jit(solution)/shard_map/all_to_all | solution.py:54
  60.1 25.7 %all-gather.1 = f32[128,1664]{1,0:T(8,128)S(1)} all-gather(f32[32,1664]{1,0:T(8,128)S(1)} %slice.62), channel_id=3, replica_groups={{0,128,256,384},{32,160,288,416},{64,192,320,448},{96,224,352,480},{1,1..., dimensions={0}, use_global_device_ids=true | all-gather | bytes 1064960 | tf_op jit(solution)/shard_map/all_gather | solution.py:62
  85.9 1.8 broadcast_in_dim.11
  87.9 5.2 %all-to-all-start.1 = ((f32[4,96,1664]{2,1,0:T(8,128)}), f32[4,96,1664]{2,1,0:T(8,128)S(1)}, u32[]{:S(2)}, u32[]{:S(2)}) async-start(f32[4,96,1664]{2,1,0:T(8,128)} %broadcast_in_dim.11), calls=%async_computation.1 | async-start | bytes 5111808 | tf_op jit(solution)/shard_map/all_to_all | solution.py:54
  93.1 27.2 %all-gather = f32[128,1536]{1,0:T(8,128)S(1)} all-gather(f32[32,1536]{1,0:T(8,128)S(1)} %slice.61), channel_id=2, replica_groups={{0,128,256,384},{32,160,288,416},{64,192,320,448},{96,224,352,480},{1,1..., dimensions={0}, use_global_device_ids=true | all-gather | bytes 983040 | tf_op jit(solution)/shard_map/all_gather | solution.py:62
  121.5 5.2 %collective-permute-start.2 = (f32[96,1536]{1,0:T(8,128)S(1)}, f32[96,1536]{1,0:T(8,128)S(1)}, u32[]{:S(2)}, u32[]{:S(2)}) collective-permute-start(f32[96,1536]{1,0:T(8,128)S(1)} %get-tuple-element.28), channel_id=1, source_target_pairs={{0,96},{32,0},{64,32},{96,64},{128,224},{160,128},{192,160},{224,1... | collective-permute-start | bytes 1769480 | tf_op jit(solution)/shard_map/ppermute | solution.py:17
  126.7 3.8 %collective-permute-start.3 = (f32[96,1536]{1,0:T(8,128)S(1)}, f32[96,1536]{1,0:T(8,128)S(1)}, u32[]{:S(2)}, u32[]{:S(2)}) collective-permute-start(f32[96,1536]{1,0:T(8,128)S(1)} %get-tuple-element.28), channel_id=1, source_target_pairs={{0,32},{32,64},{64,96},{96,0},{128,160},{160,192},{192,224},{224,1... | collective-permute-start | bytes 1769480 | tf_op jit(solution)/shard_map/ppermute | solution.py:17
  130.6 4.5 %fusion = f32[4,32,320]{2,1,0:T(8,128)S(1)} fusion(f32[4,32,3200]{2,1,0:T(8,128)S(1)} %copy-done.2, f32[320,3200]{1,0:T(8,128)} %param.4), kind=kOutput, calls=%fused_computation | convolution fusion | flops 786432000 | bytes 5898240 | tf_op jit(solution)/shard_map/dot_general | solution.py:82
  135.1 2.3 %fusion.2 = f32[4,96,320]{2,1,0:T(8,128)S(1)} fusion(f32[4,96,1664]{2,1,0:T(8,128)S(1)} %all-to-all-done.1, f32[320,3200]{1,0:T(8,128)S(1)} %copy-done), kind=kOutput, calls=%fused_computation.2 | convolution fusion | flops 1226833920 | bytes 5177344 | tf_op jit(solution)/shard_map/dot_general | solution.py:82
  138.4 2.3 %collective-permute-start.5 = (f32[48,1536]{1,0:T(8,128)S(1)}, f32[48,1536]{1,0:T(8,128)S(1)}, u32[]{:S(2)}, u32[]{:S(2)}) collective-permute-start(f32[48,1536]{1,0:T(8,128)S(1)} %slice.66), channel_id=1, source_target_pairs={{0,96},{32,0},{64,32},{96,64},{128,224},{160,128},{192,160},{224,1... | collective-permute-start | bytes 884744 | tf_op jit(solution)/shard_map/ppermute | solution.py:17
  140.7 4.9 %collective-permute-start.4 = (f32[48,1536]{1,0:T(8,128)S(1)}, f32[48,1536]{1,0:T(8,128)S(1)}, u32[]{:S(2)}, u32[]{:S(2)}) collective-permute-start(f32[48,1536]{1,0:T(8,128)S(1)} %slice.65), channel_id=1, source_target_pairs={{0,32},{32,64},{64,96},{96,0},{128,160},{160,192},{192,224},{224,1... | collective-permute-start | bytes 884744 | tf_op jit(solution)/shard_map/ppermute | solution.py:17
  145.7 1.6 fusion.7
  148.3 2.2 %collective-permute-done.4 = f32[48,1536]{1,0:T(8,128)S(1)} collective-permute-done((f32[48,1536]{1,0:T(8,128)S(1)}, f32[48,1536]{1,0:T(8,128)S(1)}, u32[]{:S(2)}, u32[]{:S(2)}) %collective-permute-start.4) | collective-permute-done | bytes 294944 | tf_op jit(solution)/shard_map/ppermute | solution.py:17
  150.5 1.1 constant_dynamic-update-slice_fusion.1
  151.9 1.9 collective-permute-start.6
  153.9 1.7 collective-permute-done.6
  155.6 31.3 %all_to_all.15 = f32[8,32,320]{2,1,0:T(8,128)S(1)} all-to-all(f32[8,32,320]{2,1,0:T(8,128)S(1)} %bitcast.60), channel_id=1, replica_groups={{0,2,4,6,8,10,12,14},{1,3,5,7,9,11,13,15},{16,18,20,22,24,26,28,30},{17..., dimensions={0} | all-to-all | bytes 655360 | tf_op jit(solution)/shard_map/all_to_all | solution.py:113
  187.0 1.9 collective-permute-start.7
  189.0 5.5 %collective-permute-done.7 = f32[32,320]{1,0:T(8,128)S(1)} collective-permute-done((f32[32,320]{1,0:T(8,128)S(1)}, f32[32,320]{1,0:T(8,128)S(1)}, u32[]{:S(2)}, u32[]{:S(2)}) %collective-permute-start.7) | collective-permute-done | bytes 40992 | tf_op jit(solution)/shard_map/ppermute | solution.py:21
  (39 shorter events, 5.8 us)
Async XLA Ops:
  1.0 29.7 %collective-permute-start = (f32[32,3200]{1,0:T(8,128)S(1)}, f32[32,3200]{1,0:T(8,128)S(1)}, u32[]{:S(2)}, u32[]{:S(2)}) collective-permute-start(f32[32,3200]{1,0:T(8,128)S(1)} %constant_dynamic-slice_fusion), channel_id=1, source_target_pairs={{0,256},{32,288},{64,320},{96,352},{128,384},{160,416},{192,448},{... | collective-permute-start | bytes 1228808 | tf_op jit(solution)/shard_map/ppermute | solution.py:13
  16.8 1.3 collective-permute-start.1
  33.6 52.3 %all-to-all-start = ((f32[4,32,3200]{2,1,0:T(8,128)}), f32[4,32,3200]{2,1,0:T(8,128)S(1)}, u32[]{:S(2)}, u32[]{:S(2)}) async-start(f32[4,32,3200]{2,1,0:T(8,128)} %broadcast_in_dim.10), calls=%async_computation | async-start | bytes 3276800 | tf_op jit(solution)/shard_map/all_to_all | solution.py:54
  85.9 2.0 %copy-start.1 = (f32[4,32,3200]{2,1,0:T(8,128)}, f32[4,32,3200]{2,1,0:T(8,128)S(1)}, u32[]{:S(2)}) copy-start(f32[4,32,3200]{2,1,0:T(8,128)S(1)} %all-to-all-done) | copy-start | bytes 4915204
  87.9 33.4 %all-to-all-start.1 = ((f32[4,96,1664]{2,1,0:T(8,128)}), f32[4,96,1664]{2,1,0:T(8,128)S(1)}, u32[]{:S(2)}, u32[]{:S(2)}) async-start(f32[4,96,1664]{2,1,0:T(8,128)} %broadcast_in_dim.11), calls=%async_computation.1 | async-start | bytes 5111808 | tf_op jit(solution)/shard_map/all_to_all | solution.py:54
  121.3 9.3 %copy-start.2 = (f32[4,32,3200]{2,1,0:T(8,128)S(1)}, f32[4,32,3200]{2,1,0:T(8,128)}, u32[]{:S(2)}) copy-start(f32[4,32,3200]{2,1,0:T(8,128)} %copy-done.1) | copy-start | bytes 4915204
  121.5 13.6 %copy-start = (f32[320,3200]{1,0:T(8,128)S(1)}, f32[320,3200]{1,0:T(8,128)}, u32[]{:S(2)}) copy-start(f32[320,3200]{1,0:T(8,128)} %param.4) | copy-start | bytes 12288004
  121.5 16.9 %collective-permute-start.2 = (f32[96,1536]{1,0:T(8,128)S(1)}, f32[96,1536]{1,0:T(8,128)S(1)}, u32[]{:S(2)}, u32[]{:S(2)}) collective-permute-start(f32[96,1536]{1,0:T(8,128)S(1)} %get-tuple-element.28), channel_id=1, source_target_pairs={{0,96},{32,0},{64,32},{96,64},{128,224},{160,128},{192,160},{224,1... | collective-permute-start | bytes 1769480 | tf_op jit(solution)/shard_map/ppermute | solution.py:17
  126.7 13.9 %collective-permute-start.3 = (f32[96,1536]{1,0:T(8,128)S(1)}, f32[96,1536]{1,0:T(8,128)S(1)}, u32[]{:S(2)}, u32[]{:S(2)}) collective-permute-start(f32[96,1536]{1,0:T(8,128)S(1)} %get-tuple-element.28), channel_id=1, source_target_pairs={{0,32},{32,64},{64,96},{96,0},{128,160},{160,192},{192,224},{224,1... | collective-permute-start | bytes 1769480 | tf_op jit(solution)/shard_map/ppermute | solution.py:17
  138.4 9.9 %collective-permute-start.5 = (f32[48,1536]{1,0:T(8,128)S(1)}, f32[48,1536]{1,0:T(8,128)S(1)}, u32[]{:S(2)}, u32[]{:S(2)}) collective-permute-start(f32[48,1536]{1,0:T(8,128)S(1)} %slice.66), channel_id=1, source_target_pairs={{0,96},{32,0},{64,32},{96,64},{128,224},{160,128},{192,160},{224,1... | collective-permute-start | bytes 884744 | tf_op jit(solution)/shard_map/ppermute | solution.py:17
  140.7 9.8 %collective-permute-start.4 = (f32[48,1536]{1,0:T(8,128)S(1)}, f32[48,1536]{1,0:T(8,128)S(1)}, u32[]{:S(2)}, u32[]{:S(2)}) collective-permute-start(f32[48,1536]{1,0:T(8,128)S(1)} %slice.65), channel_id=1, source_target_pairs={{0,32},{32,64},{64,96},{96,0},{128,160},{160,192},{192,224},{224,1... | collective-permute-start | bytes 884744 | tf_op jit(solution)/shard_map/ppermute | solution.py:17
  151.9 37.0 %copy-start.3 = (s32[32]{0:T(128)S(1)}, s32[32]{0:T(128)}, u32[]{:S(2)}) copy-start(s32[32]{0:T(128)} %param.5) | copy-start | bytes 388
  151.9 3.6 %collective-permute-start.6 = (f32[2,4,32,320]{3,2,1,0:T(8,128)S(1)}, f32[2,4,32,320]{3,2,1,0:T(8,128)S(1)}, u32[]{:S(2)}, u32[]{:S(2)}) collective-permute-start(f32[2,4,32,320]{3,2,1,0:T(8,128)S(1)} %pad_maximum_fusion.3), channel_id=1, source_target_pairs={{0,1},{1,0},{2,3},{3,2},{4,5},{5,4},{6,7},{7,6},{8,9},{9,8},{10,11... | collective-permute-start | bytes 983048 | tf_op jit(solution)/shard_map/ppermute | solution.py:30
  187.0 7.5 %collective-permute-start.7 = (f32[32,320]{1,0:T(8,128)S(1)}, f32[32,320]{1,0:T(8,128)S(1)}, u32[]{:S(2)}, u32[]{:S(2)}) collective-permute-start(f32[32,320]{1,0:T(8,128)S(1)} %reduce_sum.9), channel_id=1, source_target_pairs={{0,16},{1,17},{2,18},{3,19},{4,20},{5,21},{6,22},{7,23},{8,24},{9,... | collective-permute-start | bytes 122888 | tf_op jit(solution)/shard_map/ppermute | solution.py:21
